TPU v7x, 32 devices: a whole 2x2x4 slice. The times are simulated.
32 devices in a mesh: snp: 2 (over y), samp: 16 (over z, x, core).
Axes of the slice: x: 2, y: 2, z: 4, core: 2. Of those that a mesh axis runs over, the one named last changes fastest.
Arguments:
- dosages: bfloat16 [12288, 1024], P('samp', 'snp'), may hold values from 0 to 2
- residual: float32 [12288], P('samp'), may hold values from -40 to 40
- pair_list: int32 [4, 2], replicated, may hold values from 0 to 3, as said below
- block_slot: int32 [4], replicated, may hold values from 0 to 3, as said below
- pair_counts: int32 [4], replicated, may hold values from 3072 to 12288, as said below
Outputs:
- epistasis_score: float32 [1024], P('snp')
Inputs may be any that keep to these rules, and one draw needn't show every extreme that they name: `pair_list`: block b is paired with block (b + 1) mod 4, each such pair listed once, in some order and orientation. Counting each pair at the snp group block_slot[first block] // 2, no group gets more than 4 pairs and one group gets exactly 4. A permutation: block b is stored in columns block_slot[b] * 256 onward, on snp group block_slot[b] // 2. Pair p uses the samples with index below pair_counts[p]; some pair uses all 12288.
All inputs are finite; a program needn't handle non-finite values.
Results may differ from a plain program's by a relative error of at most 0.0021.
Values may be sent and summed in bfloat16 or wider, within the bound.
A program may use at most 64 MiB of HBM per device.

v0:
```python
import math
import jax
import jax.numpy as jnp
from jax import lax
from jax.sharding import PartitionSpec as P

BLOCK = 256


def on_device(dosages, residual, pair_list, block_slot, pair_counts):
    local_rows = dosages.shape[0]
    groups = lax.axis_size("snp")
    shards = lax.axis_size("samp")
    total_rows = local_rows * shards
    blocks = block_slot.shape[0]
    num_pairs = pair_list.shape[0]
    highest = lax.Precision.HIGHEST
    gathered = lax.all_gather(dosages, "snp", axis=1, tiled=True)
    spread_sum = lax.psum(jnp.sum(residual * residual), "samp")
    spread_var = spread_sum / total_rows
    position = lax.axis_index("samp") * local_rows + jnp.arange(local_rows, dtype=jnp.int32)
    block_ids = jnp.arange(blocks, dtype=jnp.int32)
    slot_first = jnp.sum(
        (pair_list[:, 0:1] == block_ids[None, :]).astype(jnp.int32) * block_slot[None, :], axis=1
    )
    slot_second = jnp.sum(
        (pair_list[:, 1:2] == block_ids[None, :]).astype(jnp.int32) * block_slot[None, :], axis=1
    )
    group_id = lax.axis_index("snp")
    pair_ids = jnp.arange(num_pairs, dtype=jnp.int32)
    width_slots = (num_pairs + groups - 1) // groups
    wanted = group_id * width_slots + jnp.arange(width_slots, dtype=jnp.int32)
    picked = (pair_ids[:, None] == wanted[None, :]).astype(jnp.int32)
    live_slot = jnp.sum(picked, axis=0)
    first_at = jnp.sum(picked * slot_first[:, None], axis=0)
    second_at = jnp.sum(picked * slot_second[:, None], axis=0)
    count_at = jnp.sum(picked * pair_counts[:, None], axis=0)
    live_rows = (position[None, :] < count_at[:, None]).astype(jnp.float32) * live_slot[
        :, None
    ].astype(jnp.float32)
    weight_rows = residual[None, :] * live_rows

    def masked_block(operand):
        second_slot, live = operand
        right = lax.dynamic_slice_in_dim(gathered, second_slot * BLOCK, BLOCK, 1)
        right_sq = right * right
        return (right_sq.astype(jnp.float32) * live[:, None]).astype(jnp.bfloat16)

    masked = lax.map(masked_block, (second_at, live_rows))
    rows = BLOCK // shards

    def one_slot(slot, buffer):
        first_col = lax.dynamic_index_in_dim(first_at, slot, 0, keepdims=False) * BLOCK
        second_col = lax.dynamic_index_in_dim(second_at, slot, 0, keepdims=False) * BLOCK
        left = lax.dynamic_slice_in_dim(gathered, first_col, rows * lax.axis_size("samp"), 1)
        right = lax.dynamic_slice_in_dim(gathered, second_col, BLOCK, 1)
        row_weight = lax.dynamic_index_in_dim(weight_rows, slot, 0, keepdims=False)
        masked_slot = lax.dynamic_index_in_dim(masked, slot, 0, keepdims=False)
        weighted = (left.astype(jnp.float32) * row_weight[:, None]).astype(jnp.bfloat16)
        left_sq = left * left
        cross = jnp.einsum("si,sj->ij", weighted, right, preferred_element_type=jnp.float32)
        moment = jnp.einsum("si,sj->ij", left_sq, masked_slot, preferred_element_type=jnp.float32)
        stacked = jnp.stack([cross, moment], axis=1)[:, :, None, :]
        return lax.dynamic_update_slice_in_dim(buffer, stacked, slot, 2)

    start_buffer = jnp.zeros((rows * lax.axis_size("samp"), 2, width_slots, BLOCK), jnp.float32)
    shares = lax.psum_scatter(
        lax.fori_loop(0, width_slots, one_slot, start_buffer),
        "samp",
        scatter_dimension=0,
        tiled=True,
    )
    zvalue = shares[:, 0] / jnp.sqrt(spread_var * shares[:, 1] + 1e-06)
    row_sums = jnp.sum(zvalue, axis=2)
    col_sums = jnp.sum(zvalue, axis=0)
    live_float = live_slot.astype(jnp.float32)
    first_hot = (first_at[:, None] == block_ids[None, :]).astype(jnp.float32) * live_float[:, None]
    second_hot = (second_at[:, None] == block_ids[None, :]).astype(jnp.float32) * live_float[
        :, None
    ]
    by_column = jnp.dot(second_hot.T, col_sums, precision=highest)
    by_row = jnp.dot(first_hot.T, row_sums.T, precision=highest)
    row_start = lax.axis_index("samp") * rows
    placed = lax.dynamic_update_slice_in_dim(
        jnp.zeros((blocks, BLOCK), jnp.float32), by_row, row_start, 1
    )
    partial_scores = (by_column + placed).reshape(blocks * BLOCK)
    group_part = lax.psum_scatter(partial_scores, "snp", scatter_dimension=0, tiled=True)
    totals = lax.psum(group_part, "samp")
    return totals / math.sqrt(2 * BLOCK)


def solution(mesh):
    return jax.shard_map(
        on_device,
        mesh=mesh,
        in_specs=(P("samp", "snp"), P("samp"), P(), P(), P()),
        out_specs=P("snp"),
        check_vma=False,
    )
```

profile of v0, /device:TPU:0, one launch (start us, length us, event | category | flops | bytes accessed | tf_op | source)
XLA Modules:
  0.0 156.7 jit_solution(12194418596713878061)
XLA Ops:
  6.5 0.0 all-gather.2.cloned.1.call-start
  6.5 0.7 all-gather.2.cloned.1.call-update
  7.3 0.0 reduce-scatter.2.cloned.1.call-start
  7.3 0.8 slice_bitcast_fusion
  8.1 0.9 select_reduce_fusion.1
  9.0 0.9 select_reduce_fusion.4
  9.9 0.8 compare_select_fusion
  10.6 28.2 %all-gather.2.cloned.1.call-done = bf16[768,1024]{1,0:T(8,128)(2,1)} async-done(((bf16[768,512]{1,0:T(8,128)(2,1)}), bf16[768,1024]{1,0:T(8,128)(2,1)}) %all-gather.2.cloned.1.call-update) | async-done | bytes 1572880 | tf_op jit(solution)/shard_map/all_gather | solution.py:18
  38.8 4.9 %while.23 = (s32[]{:T(128)}, bf16[2,768,256]{2,1,0:T(8,128)(2,1)S(1)}, s32[2]{0:T(128)S(1)}, bf16[768,1024]{1,0:T(8,128)(2,1)}, f32[2,768]{1,0:T(2,128)S(1)}, /*...) while((s32[]{:T(128)}, bf16[2,768,256]{2,1,0:T(8,128)(2,1)S(1)}, s32[2]{0:T(128)S(1)}, ...), condition=%wide.region_7.0_spmd, body=%wide.region_6.0_spmd.sunk | while | flops 983046 | bytes 796835 | solution.py:49
  38.8 0.6 dynamic_slice.85
  40.1 1.2 fusion.35
  41.3 0.6 dynamic_slice.85
  42.5 1.2 fusion.35
  43.7 0.0 copy-start.1
  43.7 0.0 copy-start.2
  43.8 11.0 %while.24 = (s32[]{:T(128)}, f32[256,2,2,256]{3,0,1,2:T(8,128)S(1)}, s32[2]{0:T(128)S(1)}, bf16[768,1024]{1,0:T(8,128)(2,1)}, f32[2,768]{1,0:T(2,128)S(1)}, /*in...) while((s32[]{:T(128)}, ...), condition=%wide.region_9.10_spmd, body=%wide.region_8.9_spmd.sunk | while | flops 202637312 | bytes 3155701 | solution.py:68
  43.8 0.6 dynamic_slice.91
  45.0 0.6 dynamic_slice.92
  46.3 1.6 %convolution_bitcast_fusion.5 = f32[256,1,256]{2,0,1:T(8,128)S(1)} fusion(bf16[768,1024]{1,0:T(8,128)(2,1)} %get-tuple-element.320, s32[]{:T(128)S(6)} %select_n.38, f32[768]{0:T(1024)S(1)} %dynamic-slice_reduce_fusion.5, s32[]{:T(128)S(6)} %select_n.37), kind=kOutput, calls=%fused_computation.5.clone.1 | convolution fusion | flops 101253120 | bytes 1051656 | tf_op jit(solution)/shard_map/while/body/eval_jaxpr/si,sj->ij/dot_general | solution.py:61
  47.9 1.3 convolution_bitcast_fusion.4
  49.3 0.6 dynamic_slice.91
  50.5 0.6 dynamic_slice.92
  51.7 1.6 %convolution_bitcast_fusion.5 = f32[256,1,256]{2,0,1:T(8,128)S(1)} fusion(bf16[768,1024]{1,0:T(8,128)(2,1)} %get-tuple-element.320, s32[]{:T(128)S(6)} %select_n.38, f32[768]{0:T(1024)S(1)} %dynamic-slice_reduce_fusion.5, s32[]{:T(128)S(6)} %select_n.37), kind=kOutput, calls=%fused_computation.5.clone.1 | convolution fusion | flops 101253120 | bytes 1051656 | tf_op jit(solution)/shard_map/while/body/eval_jaxpr/si,sj->ij/dot_general | solution.py:61
  53.3 1.3 convolution_bitcast_fusion.4
  54.7 0.0 copy-start
  54.7 1.0 copy-done
  55.7 0.0 reduce-scatter.2.cloned.1.call-update
  55.7 0.0 copy-done.1
  55.7 0.6 multiply_reduce_fusion
  56.3 33.9 %psum.14 = f32[]{:T(128)} all-reduce(f32[]{:T(128)} %multiply_reduce_fusion), channel_id=1, replica_groups=mesh['snp'=2,'samp'=16] {'samp'}, use_global_device_ids=true, to_apply=%region_12.13 | all-reduce | flops 1 | bytes 8 | tf_op jit(solution)/shard_map/psum | solution.py:19
  90.9 0.0 copy-done.2
  90.9 0.6 dynamic-slice.1
  92.1 21.1 %reduce-scatter.2.cloned.1.call-done = f32[16,2,2,256]{3,0,1,2:T(8,128)} async-done(((f32[256,2,2,256]{3,0,1,2:T(8,128)}), f32[16,2,2,256]{3,0,1,2:T(8,128)}) %reduce-scatter.2.cloned.1.call-update) | async-done | bytes 65552 | tf_op jit(solution)/shard_map/reduce_scatter | solution.py:67
  113.3 0.9 fusion.15
  114.1 0.3 fusion.17
  114.4 0.3 convolution_add_fusion
  114.6 0.1 add.97
  114.8 4.9 %all-reduce = f32[1024]{0:T(1024)S(1)} all-reduce(f32[1024]{0:T(1024)S(1)} %bitcast.43), channel_id=3, replica_groups=mesh['snp'=2,'samp'=16] {'snp'}, use_global_device_ids=true, to_apply=%region_15.16.clone | all-reduce | flops 1024 | bytes 8192
  119.7 0.1 dynamic-slice.2
  119.8 29.5 %psum.15 = f32[512]{0:T(512)S(1)} all-reduce(f32[512]{0:T(512)S(1)} %dynamic-slice.2), channel_id=1, replica_groups=mesh['snp'=2,'samp'=16] {'samp'}, use_global_device_ids=true, to_apply=%region_16.17 | all-reduce | flops 512 | bytes 4096 | tf_op jit(solution)/shard_map/psum | solution.py:89
  149.3 0.6 broadcast_multiply_fusion.1
  (12 shorter events, 0.2 us)
Async XLA Ops:
  6.5 32.3 %all-gather.2.cloned.1.call-start = ((), (), s32[]{:S(2)}) async-start(), calls=%async_computation.1 | async-start | bytes 2359296 | tf_op jit(solution)/shard_map/all_gather | solution.py:18
  7.3 106.0 %reduce-scatter.2.cloned.1.call-start = ((), (), s32[]{:S(2)}) async-start(), calls=%async_computation.2 | async-start | bytes 1114112 | tf_op jit(solution)/shard_map/reduce_scatter | solution.py:67
  43.7 12.0 %copy-start.1 = (f32[768]{0:T(1024)S(1)}, f32[768]{0:T(1024)}, u32[]{:S(2)}) copy-start(f32[768]{0:T(1024)} %param.10) | copy-start | bytes 9220
  43.7 47.1 %copy-start.2 = (u32[32]{0:T(128)S(1)}, u32[32]{0:T(128)}, u32[]{:S(2)}) copy-start(u32[32]{0:T(128)} %constant.108) | copy-start | bytes 388
  54.7 1.0 copy-start
Sparse Core Ops, SparseCore 0:
  8.9 29.8 all-gather.1
  55.9 57.3 reduce-scatter.1
where the time goes:
time: 157 us
  blocking collectives  68.3 us (44%)
  waiting for transfers between devices  50.1 us (32%)
  between operations  14.8 us (9%)
  other arithmetic  7 us (4%)
  matrix products  6.34 us (4%)
  local copies, waits for them, and re-layouts  6.29 us (4%)
  loops' own time  3.83 us (2%)
    psum x1, blocking collectives, on_device(): spread_sum = lax.psum(jnp.sum(residual * residual), 'samp')  33.9 us
    psum x1, blocking collectives, on_device(): totals = lax.psum(group_part, 'samp')  29.5 us
    all_gather x1, waiting for transfers between devices, on_device(): gathered = lax.all_gather(dosages, 'snp', axis=1, tiled=True)  28.2 us
    reduce_scatter x1, waiting for transfers between devices, on_device(): lax.psum_scatter(lax.fori_loop(0, width_slots, one_slot, start_buffer), '...  21.1 us
    unnamed x1, blocking collectives  4.95 us
    dot_general x2, matrix products, one_slot(): jnp.einsum('si,sj->ij', weighted, right, preferred_element_type=jnp.float32)  3.19 us
  transfers between devices with their start and end apart: 2, of which 2 were waited for; matrix products, arithmetic and copies ran while one was open for 3% of the time, Pallas kernels for 0%

commit v1 on v0

--- a/solution.py
+++ b/solution.py
@@ -86,7 +86,8 @@
     )
     partial_scores = (by_column + placed).reshape(blocks * BLOCK)
     group_part = lax.psum_scatter(partial_scores, "snp", scatter_dimension=0, tiled=True)
-    totals = lax.psum(group_part, "samp")
+    parts = lax.all_gather(group_part, "samp", axis=0, tiled=False)
+    totals = parts.sum(axis=0)
     return totals / math.sqrt(2 * BLOCK)
 
 

time: 157 us -> 147 us (0.936)
  blocking collectives: 68.3 us -> 58.4 us
    psum x1 -> x0, blocking collectives: 29.5 us -> none  [on_device(): totals = lax.psum(group_part, 'samp')]
    all_gather x0 -> x1, blocking collectives: none -> 19.6 us  [on_device(): parts = lax.all_gather(group_part, 'samp', axis=0, tiled=False)]
where the time goes in v1:
time: 147 us
  blocking collectives  58.4 us (40%)
  waiting for transfers between devices  50.1 us (34%)
  between operations  14.8 us (10%)
  other arithmetic  7.05 us (5%)
  matrix products  6.34 us (4%)
  local copies, waits for them, and re-layouts  6.29 us (4%)
  loops' own time  3.83 us (3%)
    psum x1, blocking collectives, on_device(): spread_sum = lax.psum(jnp.sum(residual * residual), 'samp')  33.9 us
    all_gather x1, waiting for transfers between devices, on_device(): gathered = lax.all_gather(dosages, 'snp', axis=1, tiled=True)  28.2 us
    reduce_scatter x1, waiting for transfers between devices, on_device(): lax.psum_scatter(lax.fori_loop(0, width_slots, one_slot, start_buffer), '...  21.1 us
    all_gather x1, blocking collectives, on_device(): parts = lax.all_gather(group_part, 'samp', axis=0, tiled=False)  19.6 us
    unnamed x1, blocking collectives  4.95 us
    dot_general x2, matrix products, one_slot(): jnp.einsum('si,sj->ij', weighted, right, preferred_element_type=jnp.float32)  3.19 us
  transfers between devices with their start and end apart: 2, of which 2 were waited for; matrix products, arithmetic and copies ran while one was open for 3% of the time, Pallas kernels for 0%

profile of v1, /device:TPU:0, one launch (start us, length us, event | category | flops | bytes accessed | tf_op | source)
XLA Modules:
  0.0 146.9 jit_solution(11571138887602071575)
XLA Ops:
  6.5 0.0 all-gather.4.cloned.1.call-start
  6.5 0.7 all-gather.4.cloned.1.call-update
  7.3 0.0 reduce-scatter.2.cloned.1.call-start
  7.3 0.8 slice_bitcast_fusion
  8.1 0.9 select_reduce_fusion.1
  9.0 0.9 select_reduce_fusion.4
  9.9 0.8 compare_select_fusion
  10.6 28.2 %all-gather.4.cloned.1.call-done = bf16[768,1024]{1,0:T(8,128)(2,1)} async-done(((bf16[768,512]{1,0:T(8,128)(2,1)}), bf16[768,1024]{1,0:T(8,128)(2,1)}) %all-gather.4.cloned.1.call-update) | async-done | bytes 1572880 | tf_op jit(solution)/shard_map/all_gather | solution.py:18
  38.8 4.9 %while.23 = (s32[]{:T(128)}, bf16[2,768,256]{2,1,0:T(8,128)(2,1)S(1)}, s32[2]{0:T(128)S(1)}, bf16[768,1024]{1,0:T(8,128)(2,1)}, f32[2,768]{1,0:T(2,128)S(1)}, /*...) while((s32[]{:T(128)}, bf16[2,768,256]{2,1,0:T(8,128)(2,1)S(1)}, s32[2]{0:T(128)S(1)}, ...), condition=%wide.region_7.0_spmd, body=%wide.region_6.0_spmd.sunk | while | flops 983046 | bytes 796835 | solution.py:49
  38.8 0.6 dynamic_slice.85
  40.1 1.2 fusion.35
  41.3 0.6 dynamic_slice.85
  42.5 1.2 fusion.35
  43.7 0.0 copy-start.1
  43.7 0.0 copy-start.2
  43.8 11.0 %while.24 = (s32[]{:T(128)}, f32[256,2,2,256]{3,0,1,2:T(8,128)S(1)}, s32[2]{0:T(128)S(1)}, bf16[768,1024]{1,0:T(8,128)(2,1)}, f32[2,768]{1,0:T(2,128)S(1)}, /*in...) while((s32[]{:T(128)}, ...), condition=%wide.region_9.10_spmd, body=%wide.region_8.9_spmd.sunk | while | flops 202637312 | bytes 3155701 | solution.py:68
  43.8 0.6 dynamic_slice.91
  45.0 0.6 dynamic_slice.92
  46.3 1.6 %convolution_bitcast_fusion.5 = f32[256,1,256]{2,0,1:T(8,128)S(1)} fusion(bf16[768,1024]{1,0:T(8,128)(2,1)} %get-tuple-element.320, s32[]{:T(128)S(6)} %select_n.38, f32[768]{0:T(1024)S(1)} %dynamic-slice_reduce_fusion.5, s32[]{:T(128)S(6)} %select_n.37), kind=kOutput, calls=%fused_computation.5.clone.1 | convolution fusion | flops 101253120 | bytes 1051656 | tf_op jit(solution)/shard_map/while/body/eval_jaxpr/si,sj->ij/dot_general | solution.py:61
  47.9 1.3 convolution_bitcast_fusion.4
  49.3 0.6 dynamic_slice.91
  50.5 0.6 dynamic_slice.92
  51.7 1.6 %convolution_bitcast_fusion.5 = f32[256,1,256]{2,0,1:T(8,128)S(1)} fusion(bf16[768,1024]{1,0:T(8,128)(2,1)} %get-tuple-element.320, s32[]{:T(128)S(6)} %select_n.38, f32[768]{0:T(1024)S(1)} %dynamic-slice_reduce_fusion.5, s32[]{:T(128)S(6)} %select_n.37), kind=kOutput, calls=%fused_computation.5.clone.1 | convolution fusion | flops 101253120 | bytes 1051656 | tf_op jit(solution)/shard_map/while/body/eval_jaxpr/si,sj->ij/dot_general | solution.py:61
  53.3 1.3 convolution_bitcast_fusion.4
  54.7 0.0 copy-start
  54.7 1.0 copy-done
  55.7 0.0 reduce-scatter.2.cloned.1.call-update
  55.7 0.0 copy-done.1
  55.8 0.6 multiply_reduce_fusion
  56.4 33.9 %psum.7 = f32[]{:T(128)} all-reduce(f32[]{:T(128)} %multiply_reduce_fusion), channel_id=1, replica_groups=mesh['snp'=2,'samp'=16] {'samp'}, use_global_device_ids=true, to_apply=%region_12.13 | all-reduce | flops 1 | bytes 8 | tf_op jit(solution)/shard_map/psum | solution.py:19
  90.9 0.0 copy-done.2
  90.9 0.6 dynamic-slice.1
  92.1 21.1 %reduce-scatter.2.cloned.1.call-done = f32[16,2,2,256]{3,0,1,2:T(8,128)} async-done(((f32[256,2,2,256]{3,0,1,2:T(8,128)}), f32[16,2,2,256]{3,0,1,2:T(8,128)}) %reduce-scatter.2.cloned.1.call-update) | async-done | bytes 65552 | tf_op jit(solution)/shard_map/reduce_scatter | solution.py:67
  113.3 0.9 fusion.15
  114.1 0.3 fusion.17
  114.4 0.3 convolution_add_fusion
  114.7 0.1 add.95
  114.8 4.9 %all-reduce = f32[1024]{0:T(1024)S(1)} all-reduce(f32[1024]{0:T(1024)S(1)} %bitcast.44), channel_id=4, replica_groups=mesh['snp'=2,'samp'=16] {'snp'}, use_global_device_ids=true, to_apply=%region_15.16.clone | all-reduce | flops 1024 | bytes 8192
  119.7 0.1 dynamic-slice.2
  119.8 19.6 %all-gather.1 = f32[16,1,512]{2,1,0:T(1,128)S(1)} all-gather(f32[1,1,512]{2,1,0:T(1,128)S(1)} %bitcast.45), channel_id=2, replica_groups=mesh['snp'=2,'samp'=16] {'samp'}, dimensions={0}, use_global_device_ids=true | all-gather | bytes 34816 | tf_op jit(solution)/shard_map/all_gather | solution.py:89
  139.5 0.6 broadcast_multiply_fusion.1
  (13 shorter events, 0.2 us)
Async XLA Ops:
  6.5 32.3 %all-gather.4.cloned.1.call-start = ((), (), s32[]{:S(2)}) async-start(), calls=%async_computation.1 | async-start | bytes 2359296 | tf_op jit(solution)/shard_map/all_gather | solution.py:18
  7.3 106.0 %reduce-scatter.2.cloned.1.call-start = ((), (), s32[]{:S(2)}) async-start(), calls=%async_computation.2 | async-start | bytes 1114112 | tf_op jit(solution)/shard_map/reduce_scatter | solution.py:67
  43.7 12.0 %copy-start.1 = (f32[768]{0:T(1024)S(1)}, f32[768]{0:T(1024)}, u32[]{:S(2)}) copy-start(f32[768]{0:T(1024)} %param.10) | copy-start | bytes 9220
  43.7 47.1 %copy-start.2 = (u32[32]{0:T(128)S(1)}, u32[32]{0:T(128)}, u32[]{:S(2)}) copy-start(u32[32]{0:T(128)} %constant.108) | copy-start | bytes 388
  54.7 1.0 copy-start
Sparse Core Ops, SparseCore 0:
  8.9 29.8 all-gather.3
  55.9 57.3 reduce-scatter.1
